TPU v7x, 32 devices: a whole 2x2x4 slice. The times are simulated.
32 devices in a mesh: grp: 2 (over y), doc: 4 (over z), qry: 2 (over x), dim: 2 (over core).
Axes of the slice: x: 2, y: 2, z: 4, core: 2. Of those that a mesh axis runs over, the one named last changes fastest.
Arguments:
- queries: bfloat16 [8, 64, 32, 128], P(('grp', 'doc'), ('qry', 'dim')), parts along dimension 0, may hold values from -0.59765625 to 0.59765625
- codebook: bfloat16 [16384, 128], P(('qry', 'dim')), may hold values from -0.5 to 0.5
- bucket_values: float32 [4], replicated, may hold values from -0.12 to 0.12
- token_centroids: int32 [32768], P(('grp', 'doc')), parts along dimension 0, may hold values from 0 to 16383, as said below
- residual_codes: int32 [32768, 128], P(('grp', 'doc')), parts along dimension 0, may hold values from 0 to 3
- doc_blocks: int32 [8, 16], P(('grp', 'doc')), parts along dimension 0, may hold values from 1 to 20, 64 in all within a row
- cand_blocks: int32 [8, 4, 4, 32], P('grp', ('qry', 'dim'), 'doc'), parts along dimension 0, may hold values from 0 to 63
- cand_counts: int32 [8, 4, 4], P('grp', ('qry', 'dim'), 'doc'), parts along dimension 0, may hold values from 1 to 32, as said below
Outputs:
- scores: float32 [8, 64, 64], P('grp', ('qry', 'dim'), 'doc'), parts along dimension 0
There are 2 independent parts, one for each index of `grp`. A program takes and returns all parts, laid end to end along the dimension named above; an argument that names none is the same for every part. Nothing has to cross between parts.
Inputs may be any that keep to these rules, and one draw needn't show every extreme that they name: `doc_blocks`: each row sums to 64. Slots from cand_counts on are ignored; some entry equals 32 in every draw. `token_centroids`: in each aligned run of 1024 tokens, exactly 256 have their centroid in each aligned range of 4096 codebook rows.
All inputs are finite; a program needn't handle non-finite values.
Results may differ from a plain program's by a relative error of at most 0.0003.
Values may be sent and summed in bfloat16 or wider, within the bound.
A program may use at most 64 MiB of HBM per device.

v0:
```python
import jax
import jax.numpy as jnp
from jax import lax
from jax.sharding import PartitionSpec as P

D = 128
BLOCK = 64


norm_eps = 1e-06
floor_value = -10000.0


def from_behind(value, axis, steps):
    count = lax.axis_size(axis)
    pairs = [(source, (source + steps) % count) for source in range(count)]
    return lax.ppermute(value, axis, pairs)


def finish_tokens(centroid, my_codes, bucket_values):
    residual = jnp.zeros_like(centroid)
    for level in range(bucket_values.shape[0]):
        residual = residual + jnp.where(my_codes == level, bucket_values[level], 0.0)
    vectors = centroid + residual
    scaled = vectors / jnp.sqrt(jnp.sum(vectors * vectors, axis=-1, keepdims=True) + norm_eps)
    return scaled.astype(jnp.bfloat16)


def token_maxima(flat_q, decoded_blocks, slot_ids):
    chosen = jnp.take(decoded_blocks, slot_ids, axis=0).reshape(-1, flat_q.shape[1])
    similar = jnp.einsum("qd,nd->qn", flat_q, chosen, preferred_element_type=jnp.float32)
    return similar.reshape(flat_q.shape[0], slot_ids.shape[0], -1).max(axis=2)


def score_panel(panel_now, decoded_blocks, slot_ids, live_count, block_doc, doc_total):
    flat_q = panel_now.reshape(-1, panel_now.shape[-1])
    slot_total = slot_ids.shape[0]
    tokens_max = token_maxima(flat_q, decoded_blocks, slot_ids)
    alive_slots = jnp.arange(slot_total, dtype=jnp.int32) < live_count
    block_hits = slot_ids[:, None] == jnp.arange(block_doc.shape[0], dtype=jnp.int32)[None, :]
    slot_doc = jnp.sum(jnp.where(block_hits, block_doc[None, :], 0), axis=1)
    member = (slot_doc[:, None] == jnp.arange(doc_total, dtype=jnp.int32)[None, :]) & alive_slots[
        :, None
    ]
    best_max = jnp.max(jnp.where(member[None], tokens_max[:, :, None], floor_value), axis=1)
    present = jnp.any(member, axis=0)
    masked = jnp.where(present[None], best_max, 0.0)
    return (
        masked.reshape(panel_now.shape[0], panel_now.shape[1], doc_total).sum(axis=1)
        / panel_now.shape[1]
    )


def local(
    queries,
    codebook,
    bucket_values,
    token_centroids,
    residual_codes,
    doc_blocks,
    cand_blocks,
    cand_counts,
):
    rows_held = codebook.shape[0]
    position = lax.axis_index(("qry", "dim"))
    offset_ids = token_centroids - position * rows_held
    owned = (offset_ids >= 0) & (offset_ids < rows_held)
    picked = jnp.take(codebook, jnp.clip(offset_ids, 0, rows_held - 1), axis=0)
    row_terms = jnp.where(owned[:, None], picked.astype(jnp.float32), 0.0)
    centroid = lax.psum(row_terms.astype(jnp.bfloat16), ("qry", "dim")).astype(jnp.float32)
    decoded = finish_tokens(centroid, residual_codes, bucket_values)
    decoded_blocks = decoded.reshape(-1, BLOCK * D)
    doc_total = doc_blocks.shape[1]
    doc_ends = jnp.cumsum(doc_blocks[0])
    block_range = jnp.arange(decoded_blocks.shape[0], dtype=jnp.int32)
    block_doc = jnp.sum(doc_ends[None, :] <= block_range[:, None], axis=1)
    shards = lax.axis_size("doc")
    doc_index = lax.axis_index("doc")
    slot_table = cand_blocks[:, 0, 0, :]
    count_table = cand_counts[:, 0, 0]
    panel_size = queries.shape[1]
    totals = jnp.zeros((shards, panel_size, doc_total), jnp.float32)

    def record(acc, panel_now, source):
        slot_ids = lax.dynamic_index_in_dim(slot_table, source, 0, keepdims=False)
        live_count = lax.dynamic_index_in_dim(count_table, source, 0, keepdims=False)
        result = score_panel(panel_now, decoded_blocks, slot_ids, live_count, block_doc, doc_total)
        return lax.dynamic_update_slice(acc, result[None], (source, jnp.int32(0), jnp.int32(0)))

    def advance(s, state_pair):
        acc, panel_now = state_pair
        source = (doc_index - s) % shards
        acc = record(acc, panel_now, source)
        panel_now = from_behind(panel_now, "doc", 1)
        return (acc, panel_now)

    totals, last_panel = lax.fori_loop(0, shards - 1, advance, (totals, queries[0]))
    totals = record(totals, last_panel, (doc_index - shards + 1) % shards)
    return totals


def solution(mesh):
    in_specs = (
        P(("grp", "doc"), ("qry", "dim"), None, None),
        P(("qry", "dim"), None),
        P(),
        P(("grp", "doc")),
        P(("grp", "doc"), None),
        P(("grp", "doc"), None),
        P("grp", ("qry", "dim"), "doc", None),
        P("grp", ("qry", "dim"), "doc"),
    )
    out_specs = P("grp", ("qry", "dim"), "doc")
    return jax.shard_map(local, mesh=mesh, in_specs=in_specs, out_specs=out_specs, check_vma=False)
```

profile of v0, /device:TPU:0, one launch (start us, length us, event | category | flops | bytes accessed | tf_op | source)
XLA Modules:
  0.0 110.7 jit_solution(12907940898587436003)
XLA Ops:
  6.5 0.8 fusion.4
  7.4 0.7 compare_and_fusion.2
  8.1 14.9 %gather_fusion.1 = bf16[4096,128]{1,0:T(8,128)(2,1)} fusion(bf16[4096,128]{1,0:T(8,128)(2,1)S(1)} %copy-done, s32[4096]{0:T(1024)S(1)} %fusion.4), kind=kCustom, calls=%fused_computation.2 | custom fusion | bytes 2113536 | tf_op jit(solution)/shard_map/jit(_take)/gather | solution.py:68
  23.0 5.8 %select_convert_fusion = bf16[4096,128]{1,0:T(8,128)(2,1)} fusion(bf16[4096,128]{1,0:T(8,128)(2,1)} %gather_fusion.1, pred[4096]{0:T(1024)(128)(4,1)S(1)} %get-tuple-element.231, pred[4096]{0:T(1024)(128)(4,1)S(1)} %get-tuple-element.230), kind=kLoop, calls=%fused_computation.22 | loop fusion | flops 2097152 | bytes 2105344 | tf_op jit(solution)/shard_map/convert_element_type | solution.py:70
  31.5 36.3 %all-reduce.2.cloned.1.call-done = bf16[4096,128]{1,0:T(8,128)(2,1)} async-done(((bf16[4096,128]{1,0:T(8,128)(2,1)}), bf16[4096,128]{1,0:T(8,128)(2,1)}) %all-reduce.2.cloned.1.call-update) | async-done | bytes 1048592 | tf_op jit(solution)/shard_map/psum | solution.py:70
  67.8 4.8 %multiply_reduce_fusion = f32[4096]{0:T(1024)S(1)} fusion(f32[]{:T(128)} %bitcast.13, s32[4096,128]{1,0:T(8,128)S(1)} %copy-done.1, f32[]{:T(128)} %bitcast.12, f32[]{:T(128)} %bitcast.11, f32[]{:T(128)} %bitcast.10, bf16[4096,128]{1,0:T(8,128)(2,1)} %all-reduce.2.cloned.1.call-done), kind=kLoop, calls=%fused_computation.20 | loop fusion | flops 7860224 | bytes 3162128 | tf_op jit(solution)/shard_map/reduce_sum | solution.py:25
  72.6 4.4 %divide_convert_fusion = bf16[4096,128]{1,0:T(8,128)(2,1)} fusion(f32[4096]{0:T(1024)S(1)} %add_sqrt_fusion, f32[]{:T(128)} %bitcast.13, s32[4096,128]{1,0:T(8,128)S(1)} %copy-done.1, f32[]{:T(128)} %bitcast.12, f32[]{:T(128)} %bitcast.11, f32[]{:T(128)} %bitcast.10, bf16[4096,128]{1,0:T(8,128)(2,1)S(1)} %copy-done.3), kind=kLoop, calls=%fused_computation.19 | loop fusion | flops 7864320 | bytes 4210704 | tf_op jit(solution)/shard_map/convert_element_type | solution.py:26
  77.0 1.5 %reshape.212 = bf16[64,8192]{1,0:T(8,128)(2,1)S(1)} reshape(bf16[4096,128]{1,0:T(8,128)(2,1)} %divide_convert_fusion) | data formatting | bytes 2097152 | tf_op jit(solution)/shard_map/reshape | solution.py:72
  78.5 0.9 gather_fusion.2
  79.5 0.9 copy.19
  80.4 20.5 %while.17 = (s32[]{:T(128)}, f32[4,16,16]{2,1,0:T(8,128)S(1)}, bf16[16,32,128]{2,1,0:T(8,128)(2,1)S(1)}, s32[]{:T(128)}, s32[4,32]{1,0:T(4,128)S(1)}, /*index=5*...) while((s32[]{:T(128)}, f32[4,16,16]{2,1,0:T(8,128)S(1)}, ...), condition=%wide.region_10.12_spmd, body=%wide.region_4.11_spmd.sunk | while | flops 270271296 | bytes 4875120 | solution.py:97
  80.4 1.5 %collective-permute-start = (bf16[16,32,128]{2,1,0:T(8,128)(2,1)S(1)}, bf16[16,32,128]{2,1,0:T(8,128)(2,1)S(1)}, u32[]{:S(2)}, u32[]{:S(2)}) collective-permute-start(bf16[16,32,128]{2,1,0:T(8,128)(2,1)S(1)} %copy.37), channel_id=1, source_target_pairs={{0,4},{4,8},{8,12},{12,0},{1,5},{5,9},{9,13},{13,1},{2,6},{6,10},{... | collective-permute-start | bytes 393224 | tf_op jit(solution)/shard_map/while/body/eval_jaxpr/ppermute | solution.py:17
  82.0 0.9 gather_fusion
  83.9 0.7 iota_compare_fusion.8
  85.0 0.7 bitcast_reduce_fusion.2
  86.2 1.1 collective-permute-done
  87.8 0.9 gather_fusion
  89.8 0.7 iota_compare_fusion.8
  90.8 0.7 bitcast_reduce_fusion.2
  92.0 2.1 %collective-permute-done = bf16[16,32,128]{2,1,0:T(8,128)(2,1)S(1)} collective-permute-done((bf16[16,32,128]{2,1,0:T(8,128)(2,1)S(1)}, bf16[16,32,128]{2,1,0:T(8,128)(2,1)S(1)}, u32[]{:S(2)}, u32[]{:S(2)}) %collective-permute-start) | collective-permute-done | bytes 131104 | tf_op jit(solution)/shard_map/while/body/eval_jaxpr/ppermute | solution.py:17
  94.3 0.9 gather_fusion
  97.3 0.7 bitcast_reduce_fusion.2
  98.5 2.5 %collective-permute-done = bf16[16,32,128]{2,1,0:T(8,128)(2,1)S(1)} collective-permute-done((bf16[16,32,128]{2,1,0:T(8,128)(2,1)S(1)}, bf16[16,32,128]{2,1,0:T(8,128)(2,1)S(1)}, u32[]{:S(2)}, u32[]{:S(2)}) %collective-permute-start) | collective-permute-done | bytes 131104 | tf_op jit(solution)/shard_map/while/body/eval_jaxpr/ppermute | solution.py:17
  101.0 1.8 %convolution_reduce_fusion = f32[512,32]{0,1:T(8,128)S(1)} fusion(bf16[512,128,1]{1,0,2:T(8,128)(2,1)S(1)} %bitcast.51, bf16[32,64,128]{2,1,0:T(8,128)(2,1)} %bitcast.54), kind=kOutput, calls=%fused_computation.23 | convolution fusion | flops 269467648 | bytes 720896 | tf_op jit(solution)/shard_map/qd,nd->qn/dot_general | solution.py:31
  (85 shorter events, 10.7 us)
Async XLA Ops:
  6.5 1.6 %copy-start = (bf16[4096,128]{1,0:T(8,128)(2,1)S(1)}, bf16[4096,128]{1,0:T(8,128)(2,1)}, u32[]{:S(2)}) copy-start(bf16[4096,128]{1,0:T(8,128)(2,1)} %param.13) | copy-start | bytes 3145732
  6.5 61.3 %all-reduce.2.cloned.1.call-start = ((), (), s32[]{:S(2)}) async-start(), calls=%async_computation | async-start | bytes 2097152 | tf_op jit(solution)/shard_map/psum | solution.py:70
  23.0 5.8 %copy-start.7 = (s32[1,16]{1,0:T(1,128)S(1)}, s32[1,16]{1,0:T(1,128)}, u32[]{:S(2)}) copy-start(s32[1,16]{1,0:T(1,128)} %param.17) | copy-start | bytes 196
  23.0 6.2 %copy-start.6 = (s32[4,1,1,32]{3,2,1,0:T(1,128)S(1)}, s32[4,1,1,32]{3,2,1,0:T(1,128)}, u32[]{:S(2)}) copy-start(s32[4,1,1,32]{3,2,1,0:T(1,128)} %param.18) | copy-start | bytes 1540
  23.0 6.2 %copy-start.8 = (s32[4,1,1]{0,2,1:T(1,128)S(1)}, s32[4,1,1]{0,2,1:T(1,128)}, u32[]{:S(2)}) copy-start(s32[4,1,1]{0,2,1:T(1,128)} %param.19) | copy-start | bytes 52
  23.0 7.9 %copy-start.5 = (f32[4]{0:T(128)S(1)}, f32[4]{0:T(128)}, u32[]{:S(2)}) copy-start(f32[4]{0:T(128)} %param.14) | copy-start | bytes 52
  23.0 44.8 %copy-start.1 = (s32[4096,128]{1,0:T(8,128)S(1)}, s32[4096,128]{1,0:T(8,128)}, u32[]{:S(2)}) copy-start(s32[4096,128]{1,0:T(8,128)} %param.16) | copy-start | bytes 6291460
  67.8 4.8 %copy-start.3 = (bf16[4096,128]{1,0:T(8,128)(2,1)S(1)}, bf16[4096,128]{1,0:T(8,128)(2,1)}, u32[]{:S(2)}) copy-start(bf16[4096,128]{1,0:T(8,128)(2,1)} %all-reduce.2.cloned.1.call-done) | copy-start | bytes 3145732
  79.4 1.0 copy-start.2
  80.4 6.9 %collective-permute-start = (bf16[16,32,128]{2,1,0:T(8,128)(2,1)S(1)}, bf16[16,32,128]{2,1,0:T(8,128)(2,1)S(1)}, u32[]{:S(2)}, u32[]{:S(2)}) collective-permute-start(bf16[16,32,128]{2,1,0:T(8,128)(2,1)S(1)} %copy.37), channel_id=1, source_target_pairs={{0,4},{4,8},{8,12},{12,0},{1,5},{5,9},{9,13},{13,1},{2,6},{6,10},{... | collective-permute-start | bytes 393224 | tf_op jit(solution)/shard_map/while/body/eval_jaxpr/ppermute | solution.py:17
  87.3 6.8 %collective-permute-start = (bf16[16,32,128]{2,1,0:T(8,128)(2,1)S(1)}, bf16[16,32,128]{2,1,0:T(8,128)(2,1)S(1)}, u32[]{:S(2)}, u32[]{:S(2)}) collective-permute-start(bf16[16,32,128]{2,1,0:T(8,128)(2,1)S(1)} %copy.37), channel_id=1, source_target_pairs={{0,4},{4,8},{8,12},{12,0},{1,5},{5,9},{9,13},{13,1},{2,6},{6,10},{... | collective-permute-start | bytes 393224 | tf_op jit(solution)/shard_map/while/body/eval_jaxpr/ppermute | solution.py:17
  94.2 6.8 %collective-permute-start = (bf16[16,32,128]{2,1,0:T(8,128)(2,1)S(1)}, bf16[16,32,128]{2,1,0:T(8,128)(2,1)S(1)}, u32[]{:S(2)}, u32[]{:S(2)}) collective-permute-start(bf16[16,32,128]{2,1,0:T(8,128)(2,1)S(1)} %copy.37), channel_id=1, source_target_pairs={{0,4},{4,8},{8,12},{12,0},{1,5},{5,9},{9,13},{13,1},{2,6},{6,10},{... | collective-permute-start | bytes 393224 | tf_op jit(solution)/shard_map/while/body/eval_jaxpr/ppermute | solution.py:17
  101.0 2.2 %copy-start.4 = (f32[4,16,16]{2,1,0:T(8,128)}, f32[4,16,16]{2,1,0:T(8,128)S(1)}, u32[]{:S(2)}) copy-start(f32[4,16,16]{2,1,0:T(8,128)S(1)} %get-tuple-element.206) | copy-start | bytes 12292
Sparse Core Ops, SparseCore 0:
  28.9 38.8 all-reduce.1
where the time goes:
time: 111 us
  waiting for transfers between devices  42 us (38%)
  local copies, waits for them, and re-layouts  25.7 us (23%)
  other arithmetic  23.1 us (21%)
  between operations  13.6 us (12%)
  matrix products  3.93 us (4%)
  starting transfers between devices  2.07 us (2%)
    psum x1, waiting for transfers between devices, local(): lax.psum(row_terms.astype(jnp.bfloat16), ('qry', 'dim')).astype(jnp.float32)  36.3 us
    gather x1, local copies, waits for them, and re-layouts, local(): picked = jnp.take(codebook, jnp.clip(offset_ids, 0, rows_held - 1), axis=0)  14.9 us
    convert_element_type x1, other arithmetic, local(): row_terms.astype(jnp.bfloat16)  5.76 us
    ppermute x3, waiting for transfers between devices, from_behind(): return lax.ppermute(value, axis, pairs)  5.68 us
    reduce_sum x1, other arithmetic, finish_tokens(): jnp.sum(vectors * vectors, axis=-1, keepdims=True) + norm_eps  4.8 us
    convert_element_type x1, other arithmetic, finish_tokens(): return scaled.astype(jnp.bfloat16)  4.35 us
    dot_general x4, matrix products, token_maxima(): jnp.einsum('qd,nd->qn', flat_q, chosen, preferred_element_type=jnp.float32)  3.93 us
    gather x4, local copies, waits for them, and re-layouts, token_maxima(): jnp.take(decoded_blocks, slot_ids, axis=0).reshape(-1, flat_q.shape[1])  3.5 us
  transfers between devices with their start and end apart: 4, of which 4 were waited for; matrix products, arithmetic and copies ran while one was open for 14% of the time, Pallas kernels for 0%

commit v1 on v0

v1 whole, which is shorter than its diff:
```python
import functools

import jax
import jax.numpy as jnp
from jax import lax
from jax.experimental import pallas as pl
from jax.experimental.pallas import tpu as pltpu
from jax.sharding import PartitionSpec as P

BLOCK = 64
LANES = 128
ROWS = 8
SUPER = ROWS * LANES

norm_eps = 1e-06
floor_value = -10000.0
bf16, f32, i32 = jnp.bfloat16, jnp.float32, jnp.int32


def kernel(
    shards, owners_x, cores,
    ids_ref, cand_ref, counts_ref, docs_ref, bucket_ref, q_ref, book_hbm, codes_hbm,
    out_ref,
    book, codes, ranks, place, slots, rows, perm, resid, dec, panels, best,
    load_sem, q_send, q_recv, x_send, c_send, r_send, row_recv,
):
    y, z = lax.axis_index("grp"), lax.axis_index("doc")
    x, c = lax.axis_index("qry"), lax.axis_index("dim")
    owners = owners_x * cores
    me = x * cores + c
    held = book.shape[0]
    supers = codes.shape[0] // SUPER
    width = SUPER // owners
    run_rows = codes.shape[0] // owners // LANES
    part = SUPER // (run_rows * LANES)
    share = width // part
    token_rows = ids_ref.shape[0]

    load_book = pltpu.make_async_copy(book_hbm, book, load_sem.at[0])
    load_codes = pltpu.make_async_copy(codes_hbm, codes, load_sem.at[1])
    load_book.start()
    load_codes.start()

    barrier = pltpu.get_barrier_semaphore()
    peers = [(y, lax.rem(z + s, shards), x, c) for s in range(1, shards)]
    peers += [(y, z, lax.rem(x + s, owners_x), c) for s in range(1, owners_x)]
    peers += [(y, z, x, lax.rem(c + s, cores)) for s in range(1, cores)]
    for peer in peers:
        pl.semaphore_signal(barrier, inc=1, device_id=peer, device_id_type=pl.DeviceIdType.MESH)

    ids = ids_ref[...]
    owner = ids // held
    lane_r = lax.broadcasted_iota(i32, (LANES, LANES), 0)
    lane_c = lax.broadcasted_iota(i32, (LANES, LANES), 1)
    before = (lane_r < lane_c).astype(bf16)
    ones = jnp.ones((LANES, LANES), bf16)
    row_r = lax.broadcasted_iota(i32, (token_rows, token_rows), 0)
    row_c = lax.broadcasted_iota(i32, (token_rows, token_rows), 1)
    above = ((row_c < row_r) & (row_c // run_rows == row_r // run_rows)).astype(bf16)
    rank = jnp.zeros(ids.shape, f32)
    for o in range(owners):
        mask = (owner == o).astype(f32)
        inside = jnp.dot(mask.astype(bf16), before, preferred_element_type=f32)
        totals = jnp.dot(mask.astype(bf16), ones, preferred_element_type=f32)
        carried = jnp.dot(above, totals.astype(bf16), preferred_element_type=f32)
        rank = rank + mask * (inside + carried)
    run_of = (lax.broadcasted_iota(i32, ids.shape, 0) // run_rows) % part
    slot = run_of * share + rank.astype(i32)
    place[...] = owner * width + slot
    slots[...] = jnp.where(owner == me, slot, -1)
    ranks[...] = ids - me * held

    pl.semaphore_wait(barrier, len(peers))

    def q_copy(s):
        return pltpu.make_async_remote_copy(
            src_ref=q_ref, dst_ref=panels.at[z],
            send_sem=q_send.at[s], recv_sem=q_recv.at[z],
            device_id=(y, lax.rem(z + s, shards), x, c), device_id_type=pl.DeviceIdType.MESH,
        )

    for s in range(1, shards):
        q_copy(s).start()

    def chunk(q, o):
        return rows.at[q, pl.ds(pl.multiple_of(o * width, width), width), :]

    def send(q, o, sem, device):
        return pltpu.make_async_remote_copy(
            src_ref=chunk(q, o), dst_ref=chunk(q, o), send_sem=sem, recv_sem=row_recv.at[q, o],
            device_id=device, device_id_type=pl.DeviceIdType.MESH,
        )

    def x_copy(q, s):
        return send(q, me, x_send.at[q, s], (y, z, lax.rem(x + s, owners_x), c))

    def c_copy(q, s):
        return send(q, me, c_send.at[q, s], (y, z, x, lax.rem(c + s, cores)))

    def relay(q, s, t):
        source = lax.rem(x + s, owners_x) * cores + c
        return send(q, source, r_send.at[q, s, t], (y, z, x, lax.rem(c + t, cores)))

    load_book.wait()
    spot = lax.broadcasted_iota(i32, (width, LANES), 0)
    held_iota = lax.broadcasted_iota(i32, (width, held), 1)

    def pick(q, _):
        slot_q = slots[pl.ds(pl.multiple_of(q * ROWS, ROWS), ROWS), :]
        id_q = ranks[pl.ds(pl.multiple_of(q * ROWS, ROWS), ROWS), :]
        total = jnp.zeros((width, LANES), i32)
        for s in range(ROWS):
            total = total + jnp.where(slot_q[s:s + 1, :] == spot, id_q[s:s + 1, :], 0)
        chosen = jnp.sum(total.astype(f32), axis=1, keepdims=True).astype(i32)
        hot = jnp.where(held_iota == chosen, 1.0, 0.0).astype(bf16)
        picked = jnp.dot(hot, book[...], preferred_element_type=f32).astype(bf16)
        rows[q, pl.ds(pl.multiple_of(me * width, width), width), :] = picked
        for s in range(1, owners_x):
            x_copy(q, s).start()
        for s in range(1, cores):
            c_copy(q, s).start()
        return 0

    lax.fori_loop(0, supers, pick, 0)

    load_codes.wait()
    levels = [bucket_ref[v] for v in range(bucket_ref.shape[0])]
    place_iota = lax.broadcasted_iota(i32, (2 * ROWS, SUPER), 1)

    def prepare(q, _):
        place_q = place[pl.ds(pl.multiple_of(q * ROWS, ROWS), ROWS), :]
        for l in range(0, LANES, 2):
            pair = jnp.concatenate([place_q[:, l:l + 1], place_q[:, l + 1:l + 2]], axis=0)
            perm[q, l * ROWS:(l + 2) * ROWS, :] = jnp.where(place_iota == pair, 1.0, 0.0).astype(bf16)
        for l in range(LANES):
            code = codes[pl.ds(q * SUPER + l, ROWS, stride=LANES), :]
            value = jnp.full(code.shape, levels[0], f32)
            for v in range(1, len(levels)):
                value = jnp.where(code == v, levels[v], value)
            resid[q, l * ROWS:(l + 1) * ROWS, :] = value
        for s in range(1, owners_x):
            source = lax.rem(x + s, owners_x) * cores + c
            x_wait = send(q, source, x_send.at[q, s], (y, z, x, c))
            x_wait.wait_recv()
            for t in range(1, cores):
                relay(q, s, t).start()
        return 0

    lax.fori_loop(0, supers, prepare, 0)

    blocks = supers * 2 * ROWS
    line = lax.broadcasted_iota(i32, (blocks, 1), 0)
    block = 2 * ROWS * (line // (2 * ROWS)) + 2 * (line % ROWS) + (line // ROWS) % 2
    end = jnp.int32(0)
    doc = jnp.zeros((blocks, 1), i32)
    docs = docs_ref.shape[1]
    for d in range(docs):
        end = end + docs_ref[0, d]
        doc = doc + jnp.where(end <= block, 1, 0)

    def score(j, query, q):
        for h in range(2):
            top = None
            for p in range(0, BLOCK * ROWS, 128):
                piece = dec[q, h * BLOCK * ROWS + p:h * BLOCK * ROWS + p + 128, :]
                sim = lax.dot_general(piece, query, (((1,), (1,)), ((), ())), preferred_element_type=f32)
                sim = jnp.max(sim.reshape(-1, ROWS, sim.shape[1]), axis=0)
                top = sim if top is None else jnp.maximum(top, sim)
            best[j, pl.ds(pl.multiple_of(q * 2 * ROWS + h * ROWS, ROWS), ROWS), :] = top

    def decode(q, _):
        for s in range(owners_x):
            for t in range(cores):
                if t == 0:
                    continue
                source = lax.rem(x + s, owners_x) * cores + lax.rem(c + t, cores)
                send(q, source, c_send.at[q, t], (y, z, x, c)).wait_recv()
        vectors = jnp.dot(perm[q], rows[q], preferred_element_type=f32) + resid[q]
        squares = jnp.sum(vectors * vectors, axis=1, keepdims=True)
        dec[q] = (vectors * lax.rsqrt(squares + norm_eps)).astype(bf16)
        score(z, q_ref[...], q)
        return 0

    lax.fori_loop(0, supers, decode, 0)

    panel_rows = q_ref.shape[0]
    queries = out_ref.shape[1]
    tokens = panel_rows // queries
    gather = (
        lax.broadcasted_iota(i32, (queries, panel_rows), 1) // tokens
        == lax.broadcasted_iota(i32, (queries, panel_rows), 0)
    ).astype(f32)
    slot_count = cand_ref.shape[3]
    slot_iota = lax.broadcasted_iota(i32, (1, slot_count), 1)

    def finish(j):
        live = (cand_ref[j, 0] == block) & (slot_iota < counts_ref[j, 0, 0])
        alive = jnp.max(jnp.where(live, 1.0, 0.0), axis=1, keepdims=True) > 0.5
        which = jnp.where(alive, doc, -1)
        maxima = best[j]
        lines = []
        for d in range(docs):
            lines.append(jnp.max(jnp.where(which == d, maxima, floor_value), axis=0, keepdims=True))
        found = jnp.concatenate(lines, axis=0)
        found = jnp.where(found > 0.5 * floor_value, found, 0.0)
        total = lax.dot_general(
            gather, found, (((1,), (1,)), ((), ())),
            preferred_element_type=f32, precision=lax.Precision.HIGHEST,
        )
        out_ref[j] = total * (1.0 / tokens)

    finish(z)

    def panel(s, _):
        j = lax.rem(z + shards - s, shards)
        pltpu.make_async_remote_copy(
            src_ref=q_ref, dst_ref=panels.at[j], send_sem=q_send.at[s], recv_sem=q_recv.at[j],
            device_id=(y, z, x, c), device_id_type=pl.DeviceIdType.MESH,
        ).wait_recv()

        def each(q, _):
            score(j, panels[j], q)
            return 0

        lax.fori_loop(0, supers, each, 0)
        finish(j)
        return 0

    lax.fori_loop(1, shards, panel, 0)

    for s in range(1, shards):
        q_copy(s).wait_send()

    def drain(q, _):
        for s in range(1, owners_x):
            x_copy(q, s).wait_send()
            for t in range(1, cores):
                relay(q, s, t).wait_send()
        for s in range(1, cores):
            c_copy(q, s).wait_send()
        return 0

    lax.fori_loop(0, supers, drain, 0)


def local(shards, owners_x, cores, queries, codebook, bucket_values, token_centroids, residual_codes,
          doc_blocks, cand_blocks, cand_counts):
    count, panel, tokens, depth = queries.shape[0], queries.shape[1], queries.shape[2], queries.shape[3]
    flat_q = queries.reshape(panel * tokens, depth)
    total = token_centroids.shape[0]
    supers = total // SUPER
    held = codebook.shape[0]
    owners = owners_x * cores
    docs = doc_blocks.shape[1]
    vmem, smem = pl.BlockSpec(memory_space=pltpu.VMEM), pl.BlockSpec(memory_space=pltpu.SMEM)
    anywhere = pl.BlockSpec(memory_space=pl.ANY)
    dma = pltpu.SemaphoreType.DMA
    return pl.pallas_call(
        functools.partial(kernel, shards, owners_x, cores),
        out_shape=jax.ShapeDtypeStruct((shards, panel, docs), f32),
        in_specs=[vmem, vmem, smem, smem, smem, vmem, anywhere, anywhere],
        out_specs=vmem,
        scratch_shapes=[
            pltpu.VMEM((held, depth), bf16),
            pltpu.VMEM((total, depth), i32),
            pltpu.VMEM((total // LANES, LANES), i32),
            pltpu.VMEM((total // LANES, LANES), i32),
            pltpu.VMEM((total // LANES, LANES), i32),
            pltpu.VMEM((supers, SUPER, depth), bf16),
            pltpu.VMEM((supers, SUPER, SUPER), bf16),
            pltpu.VMEM((supers, SUPER, depth), f32),
            pltpu.VMEM((supers, SUPER, depth), bf16),
            pltpu.VMEM((shards, panel * tokens, depth), bf16),
            pltpu.VMEM((shards, total // BLOCK, panel * tokens), f32),
            dma((2,)),
            dma((shards,)),
            dma((shards,)),
            dma((supers, owners_x)),
            dma((supers, cores)),
            dma((supers, owners_x, cores)),
            dma((supers, owners)),
        ],
        compiler_params=pltpu.CompilerParams(
            collective_id=0, has_side_effects=True, vmem_limit_bytes=50 * 1024 * 1024
        ),
        name="rescore",
    )(
        token_centroids.reshape(total // LANES, LANES), cand_blocks, cand_counts, doc_blocks,
        bucket_values, flat_q, codebook, residual_codes,
    )


def solution(mesh):
    in_specs = (
        P(("grp", "doc"), ("qry", "dim"), None, None),
        P(("qry", "dim"), None),
        P(),
        P(("grp", "doc")),
        P(("grp", "doc"), None),
        P(("grp", "doc"), None),
        P("grp", ("qry", "dim"), "doc", None),
        P("grp", ("qry", "dim"), "doc"),
    )
    out_specs = P("grp", ("qry", "dim"), "doc")
    body = functools.partial(local, mesh.shape["doc"], mesh.shape["qry"], mesh.shape["dim"])
    return jax.shard_map(body, mesh=mesh, in_specs=in_specs, out_specs=out_specs, check_vma=False)
```

time: 111 us -> 36.3 us (0.33)
  waiting for transfers between devices: 42 us -> 0 us
  Pallas kernels: 0 us -> 28.2 us
  other arithmetic: 23.1 us -> 0 us
  local copies, waits for them, and re-layouts: 25.7 us -> 7.78 us
  between operations: 13.6 us -> 0.02 us
  matrix products: 3.93 us -> 0 us
  starting transfers between devices: 2.07 us -> 0 us
    psum x1 -> x0, waiting for transfers between devices: 36.3 us -> none  [local(): lax.psum(row_terms.astype(jnp.bfloat16), ('qry', 'dim')).astype(jnp.float32)]
    pallas_call x0 -> x1, Pallas kernels: none -> 28.2 us  [local(): pl.pallas_call(functools.partial(kernel, shards, owners_x, cores), out_sh...]
    gather x5 -> x0, local copies, waits for them, and re-layouts: 18.4 us -> none  [the longest x1 14.9 us: local(): picked = jnp.take(codebook, jnp.clip(offset_ids, 0, rows_held - 1), axis=0)]
    convert_element_type x2 -> x0, other arithmetic: 10.1 us -> none  [the longest x1 5.76 us: local(): row_terms.astype(jnp.bfloat16)]
    unnamed x19 -> x16, local copies, waits for them, and re-layouts: 0.95 us -> 7.78 us
    reduce_sum x10 -> x0, other arithmetic: 6.33 us -> none  [the longest x1 4.8 us: finish_tokens(): jnp.sum(vectors * vectors, axis=-1, keepdims=True) + norm_eps]
    ppermute x3 -> x0, waiting for transfers between devices: 5.68 us -> none  [from_behind(): return lax.ppermute(value, axis, pairs)]
    dot_general x4 -> x0, matrix products: 3.93 us -> none  [token_maxima(): jnp.einsum('qd,nd->qn', flat_q, chosen, preferred_element_type=jnp.float32)]
  transfers between devices with their start and end apart: 4 -> 0, of which waited for: 4 -> 0; matrix products, arithmetic and copies ran while one was open for 14% -> 0% of each run, Pallas kernels for 0% -> 0%
where the time goes in v1:
time: 36.3 us; the launch traced here: 36 us
  Pallas kernels  28.2 us (78%)
  local copies, waits for them, and re-layouts  7.78 us (21%)
    pallas_call x1, Pallas kernels, local(): pl.pallas_call(functools.partial(kernel, shards, owners_x, cores), out_sh...  28.2 us
    unnamed x16, local copies, waits for them, and re-layouts  7.78 us

profile of v1, /device:TPU:0, one launch (start us, length us, event | category | flops | bytes accessed | tf_op | source)
XLA Modules:
  0.0 36.0 jit_solution(6358498770877911257)
XLA Ops:
  0.0 0.7 %copy.9.counts_ref = s32[4,1,1]{2,1,0:T(1,128)S(1)} copy(s32[4,1,1]{0,2,1:T(1,128)} %param.15) | data formatting | bytes 32 | tf_op args[7]
  0.7 0.0 copy-start
  0.7 1.6 %copy-done = s32[4096,128]{1,0:T(8,128)S(1)} copy-done((s32[4096,128]{1,0:T(8,128)S(1)}, s32[4096,128]{1,0:T(8,128)}, u32[]{:S(2)}) %copy-start) | copy-done | bytes 2097176
  2.3 0.0 copy-start.1
  2.3 1.2 %copy-done.1 = bf16[4096,128]{1,0:T(8,128)(2,1)S(1)} copy-done((bf16[4096,128]{1,0:T(8,128)(2,1)S(1)}, bf16[4096,128]{1,0:T(8,128)(2,1)}, u32[]{:S(2)}) %copy-start.1) | copy-done | bytes 1048600
  3.6 0.0 copy-start.2
  3.6 0.9 %copy-done.2 = bf16[1,16,32,128]{3,2,1,0:T(8,128)(2,1)S(1)} copy-done((bf16[1,16,32,128]{3,2,1,0:T(8,128)(2,1)S(1)}, bf16[1,16,32,128]{3,2,1,0:T(8,128)(2,1)}, u32[]{:S(2)}) %copy-start.2) | copy-done | bytes 131096
  4.5 0.0 copy-start.3
  4.5 0.7 %copy-done.3 = s32[4096]{0:T(1024)S(1)} copy-done((s32[4096]{0:T(1024)S(1)}, s32[4096]{0:T(1024)}, u32[]{:S(2)}) %copy-start.3) | copy-done | bytes 16408
  5.2 0.0 copy-start.4
  5.2 0.7 %copy-done.4 = s32[4,1,1,32]{3,2,1,0:T(1,128)S(1)} copy-done((s32[4,1,1,32]{3,2,1,0:T(1,128)S(1)}, s32[4,1,1,32]{3,2,1,0:T(1,128)}, u32[]{:S(2)}) %copy-start.4) | copy-done | bytes 536
  5.9 0.0 copy-start.5
  5.9 0.7 %copy-done.5 = s32[1,16]{1,0:T(1,128)S(1)} copy-done((s32[1,16]{1,0:T(1,128)S(1)}, s32[1,16]{1,0:T(1,128)}, u32[]{:S(2)}) %copy-start.5) | copy-done | bytes 88
  6.5 0.0 copy-start.6
  6.5 0.7 %copy-done.6 = f32[4]{0:T(128)S(1)} copy-done((f32[4]{0:T(128)S(1)}, f32[4]{0:T(128)}, u32[]{:S(2)}) %copy-start.6) | copy-done | bytes 40
  7.2 28.2 %rescore.1 = f32[4,16,16]{2,1,0:T(8,128)S(1)} custom-call(s32[32,128]{1,0:T(8,128)S(1)} %bitcast.3, s32[4,1,1,32]{3,2,1,0:T(1,128)S(1)} %copy-done.4, s32[4,1,1]{2,1,0:T(1,128)S(1)} %copy.9.counts_ref, s32[1,16]{1,0:T(1,128)S(1)} %copy-done.5, f32[4]{0:T(128)S(1)} %copy-done.6, bf16[512,128]{1,0:T(8,128)(2,1)S(1)} %bitcast.2, ...), custom_call_target="tpu_custom_call" | custom-call | tf_op jit(solution)/shard_map/rescore/pallas_call | solution.py:258
  35.4 0.6 %copy.11 = f32[4,16,16]{2,1,0:T(8,128)} copy(f32[4,16,16]{2,1,0:T(8,128)S(1)} %rescore.1) | data formatting | bytes 8192
Async XLA Ops:
  0.7 1.6 %copy-start = (s32[4096,128]{1,0:T(8,128)S(1)}, s32[4096,128]{1,0:T(8,128)}, u32[]{:S(2)}) copy-start(s32[4096,128]{1,0:T(8,128)} %codes_hbm.1) | copy-start | bytes 6291460
  2.3 1.2 %copy-start.1 = (bf16[4096,128]{1,0:T(8,128)(2,1)S(1)}, bf16[4096,128]{1,0:T(8,128)(2,1)}, u32[]{:S(2)}) copy-start(bf16[4096,128]{1,0:T(8,128)(2,1)} %book_hbm.1) | copy-start | bytes 3145732
  3.6 0.9 %copy-start.2 = (bf16[1,16,32,128]{3,2,1,0:T(8,128)(2,1)S(1)}, bf16[1,16,32,128]{3,2,1,0:T(8,128)(2,1)}, u32[]{:S(2)}) copy-start(bf16[1,16,32,128]{3,2,1,0:T(8,128)(2,1)} %param.8) | copy-start | bytes 393220
  4.5 0.7 %copy-start.3 = (s32[4096]{0:T(1024)S(1)}, s32[4096]{0:T(1024)}, u32[]{:S(2)}) copy-start(s32[4096]{0:T(1024)} %param.11) | copy-start | bytes 49156
  5.2 0.7 %copy-start.4 = (s32[4,1,1,32]{3,2,1,0:T(1,128)S(1)}, s32[4,1,1,32]{3,2,1,0:T(1,128)}, u32[]{:S(2)}) copy-start(s32[4,1,1,32]{3,2,1,0:T(1,128)} %cand_ref.1) | copy-start | bytes 1540
  5.9 0.7 %copy-start.5 = (s32[1,16]{1,0:T(1,128)S(1)}, s32[1,16]{1,0:T(1,128)}, u32[]{:S(2)}) copy-start(s32[1,16]{1,0:T(1,128)} %docs_ref.1) | copy-start | bytes 196
  6.5 0.7 %copy-start.6 = (f32[4]{0:T(128)S(1)}, f32[4]{0:T(128)}, u32[]{:S(2)}) copy-start(f32[4]{0:T(128)} %bucket_ref.1) | copy-start | bytes 52

commit v2 on v1

--- a/solution.py
+++ b/solution.py
@@ -19,9 +19,9 @@
 
 def kernel(
     shards, owners_x, cores,
-    ids_ref, cand_ref, counts_ref, docs_ref, bucket_ref, q_ref, book_hbm, codes_hbm,
+    ids_hbm, cand_hbm, counts_hbm, docs_hbm, bucket_hbm, q_hbm, book_hbm, codes_hbm,
     out_ref,
-    book, codes, ranks, place, slots, rows, perm, resid, dec, panels, best,
+    ids_ref, cand_ref, counts_ref, docs_ref, bucket_ref, q_ref, book, codes, ranks, place, slots, rows, perm, resid, dec, panels, best,
     load_sem, q_send, q_recv, x_send, c_send, r_send, row_recv,
 ):
     y, z = lax.axis_index("grp"), lax.axis_index("doc")
@@ -36,10 +36,16 @@
     share = width // part
     token_rows = ids_ref.shape[0]
 
-    load_book = pltpu.make_async_copy(book_hbm, book, load_sem.at[0])
-    load_codes = pltpu.make_async_copy(codes_hbm, codes, load_sem.at[1])
-    load_book.start()
-    load_codes.start()
+    loads = [
+        pltpu.make_async_copy(source, target, load_sem.at[n])
+        for n, (source, target) in enumerate([
+            (ids_hbm, ids_ref), (q_hbm, q_ref), (book_hbm, book), (codes_hbm, codes), (cand_hbm, cand_ref),
+            (counts_hbm, counts_ref), (docs_hbm, docs_ref), (bucket_hbm, bucket_ref),
+        ])
+    ]
+    load_ids, load_q, load_book, load_codes = loads[:4]
+    for load in loads:
+        load.start()
 
     barrier = pltpu.get_barrier_semaphore()
     peers = [(y, lax.rem(z + s, shards), x, c) for s in range(1, shards)]
@@ -48,6 +54,7 @@
     for peer in peers:
         pl.semaphore_signal(barrier, inc=1, device_id=peer, device_id_type=pl.DeviceIdType.MESH)
 
+    load_ids.wait()
     ids = ids_ref[...]
     owner = ids // held
     lane_r = lax.broadcasted_iota(i32, (LANES, LANES), 0)
@@ -70,6 +77,7 @@
     slots[...] = jnp.where(owner == me, slot, -1)
     ranks[...] = ids - me * held
 
+    load_q.wait()
     pl.semaphore_wait(barrier, len(peers))
 
     def q_copy(s):
@@ -124,6 +132,8 @@
     lax.fori_loop(0, supers, pick, 0)
 
     load_codes.wait()
+    for load in loads[4:]:
+        load.wait()
     levels = [bucket_ref[v] for v in range(bucket_ref.shape[0])]
     place_iota = lax.broadcasted_iota(i32, (2 * ROWS, SUPER), 1)
 
@@ -194,7 +204,7 @@
     slot_iota = lax.broadcasted_iota(i32, (1, slot_count), 1)
 
     def finish(j):
-        live = (cand_ref[j, 0] == block) & (slot_iota < counts_ref[j, 0, 0])
+        live = (cand_ref[j, 0] == block) & (slot_iota < counts_ref[j])
         alive = jnp.max(jnp.where(live, 1.0, 0.0), axis=1, keepdims=True) > 0.5
         which = jnp.where(alive, doc, -1)
         maxima = best[j]
@@ -252,15 +262,20 @@
     held = codebook.shape[0]
     owners = owners_x * cores
     docs = doc_blocks.shape[1]
-    vmem, smem = pl.BlockSpec(memory_space=pltpu.VMEM), pl.BlockSpec(memory_space=pltpu.SMEM)
-    anywhere = pl.BlockSpec(memory_space=pl.ANY)
+    vmem, hbm = pl.BlockSpec(memory_space=pltpu.VMEM), pl.BlockSpec(memory_space=pltpu.HBM)
     dma = pltpu.SemaphoreType.DMA
     return pl.pallas_call(
         functools.partial(kernel, shards, owners_x, cores),
         out_shape=jax.ShapeDtypeStruct((shards, panel, docs), f32),
-        in_specs=[vmem, vmem, smem, smem, smem, vmem, anywhere, anywhere],
+        in_specs=[hbm] * 8,
         out_specs=vmem,
         scratch_shapes=[
+            pltpu.VMEM((total // LANES, LANES), i32),
+            pltpu.VMEM(cand_blocks.shape, i32),
+            pltpu.SMEM((shards,), i32),
+            pltpu.SMEM(doc_blocks.shape, i32),
+            pltpu.SMEM(bucket_values.shape, f32),
+            pltpu.VMEM((panel * tokens, depth), bf16),
             pltpu.VMEM((held, depth), bf16),
             pltpu.VMEM((total, depth), i32),
             pltpu.VMEM((total // LANES, LANES), i32),
@@ -272,7 +287,7 @@
             pltpu.VMEM((supers, SUPER, depth), bf16),
             pltpu.VMEM((shards, panel * tokens, depth), bf16),
             pltpu.VMEM((shards, total // BLOCK, panel * tokens), f32),
-            dma((2,)),
+            dma((8,)),
             dma((shards,)),
             dma((shards,)),
             dma((supers, owners_x)),
@@ -281,11 +296,11 @@
             dma((supers, owners)),
         ],
         compiler_params=pltpu.CompilerParams(
-            collective_id=0, has_side_effects=True, vmem_limit_bytes=50 * 1024 * 1024
+            collective_id=0, has_side_effects=True, vmem_limit_bytes=64 * 1024 * 1024
         ),
         name="rescore",
     )(
-        token_centroids.reshape(total // LANES, LANES), cand_blocks, cand_counts, doc_blocks,
+        token_centroids.reshape(total // LANES, LANES), cand_blocks, cand_counts.reshape(shards), doc_blocks,
         bucket_values, flat_q, codebook, residual_codes,
     )
 

time: 36.3 us -> 29.7 us (0.82)
  local copies, waits for them, and re-layouts: 7.78 us -> 1.38 us
    unnamed x16 -> x1, local copies, waits for them, and re-layouts: 7.78 us -> 1.38 us
where the time goes in v2:
time: 29.7 us; the launch traced here: 29.4 us
  Pallas kernels  28.1 us (95%)
  local copies, waits for them, and re-layouts  1.38 us (5%)
    pallas_call x1, Pallas kernels, local(): pl.pallas_call(functools.partial(kernel, shards, owners_x, cores), out_sh...  28.1 us
    unnamed x1, local copies, waits for them, and re-layouts  1.38 us

profile of v2, /device:TPU:0, one launch (start us, length us, event | category | flops | bytes accessed | tf_op | source)
XLA Modules:
  0.0 29.4 jit_solution(2161312082702845063)
XLA Ops:
  0.0 28.1 %rescore.1 = f32[4,16,16]{2,1,0:T(8,128)} custom-call(s32[32,128]{1,0:T(8,128)} %bitcast.4, s32[4,1,1,32]{3,2,1,0:T(1,128)} %cand_hbm.1, s32[4]{0:T(128)} %bitcast.5, s32[1,16]{1,0:T(1,128)} %docs_hbm.1, f32[4]{0:T(128)} %bucket_hbm.1, bf16[512,128]{1,0:T(8,128)(2,1)} %bitcast.3, bf16[4096,128]{1,0:T(8,128)(2,1)} %book_hbm.1, s32[4096,128]{1,0:T(8,128)} %codes_hbm.1), custom_call_target="tpu_custom_call" | custom-call | tf_op jit(solution)/shard_map/rescore/pallas_call | solution.py:267
  28.1 1.4 %copy.10 = f32[4,16,16]{2,1,0:T(8,128)} copy(f32[4,16,16]{2,1,0:T(8,128)} %rescore.1) | data formatting | bytes 8192

commit v3 on v2

--- a/solution.py
+++ b/solution.py
@@ -10,6 +10,7 @@
 BLOCK = 64
 LANES = 128
 ROWS = 8
+FOLD = 4
 SUPER = ROWS * LANES
 
 norm_eps = 1e-06
@@ -21,7 +22,7 @@
     shards, owners_x, cores,
     ids_hbm, cand_hbm, counts_hbm, docs_hbm, bucket_hbm, q_hbm, book_hbm, codes_hbm,
     out_ref,
-    ids_ref, cand_ref, counts_ref, docs_ref, bucket_ref, q_ref, book, codes, ranks, place, slots, rows, perm, resid, dec, panels, best,
+    ids_ref, cand_ref, counts_ref, docs_ref, bucket_ref, q_ref, book, codes, ranks, place, slots, rows, perm, quarter, resid, dec, panels, best, found,
     load_sem, q_send, q_recv, x_send, c_send, r_send, row_recv,
 ):
     y, z = lax.axis_index("grp"), lax.axis_index("doc")
@@ -53,6 +54,20 @@
     peers += [(y, z, x, lax.rem(c + s, cores)) for s in range(1, cores)]
     for peer in peers:
         pl.semaphore_signal(barrier, inc=1, device_id=peer, device_id_type=pl.DeviceIdType.MESH)
+
+    load_q.wait()
+    panels[z] = q_ref[...].T
+    pl.semaphore_wait(barrier, len(peers))
+
+    def q_copy(s):
+        return pltpu.make_async_remote_copy(
+            src_ref=panels.at[z], dst_ref=panels.at[z],
+            send_sem=q_send.at[s], recv_sem=q_recv.at[z],
+            device_id=(y, lax.rem(z + s, shards), x, c), device_id_type=pl.DeviceIdType.MESH,
+        )
+
+    for s in range(1, shards):
+        q_copy(s).start()
 
     load_ids.wait()
     ids = ids_ref[...]
@@ -77,19 +92,6 @@
     slots[...] = jnp.where(owner == me, slot, -1)
     ranks[...] = ids - me * held
 
-    load_q.wait()
-    pl.semaphore_wait(barrier, len(peers))
-
-    def q_copy(s):
-        return pltpu.make_async_remote_copy(
-            src_ref=q_ref, dst_ref=panels.at[z],
-            send_sem=q_send.at[s], recv_sem=q_recv.at[z],
-            device_id=(y, lax.rem(z + s, shards), x, c), device_id_type=pl.DeviceIdType.MESH,
-        )
-
-    for s in range(1, shards):
-        q_copy(s).start()
-
     def chunk(q, o):
         return rows.at[q, pl.ds(pl.multiple_of(o * width, width), width), :]
 
@@ -111,7 +113,19 @@
 
     load_book.wait()
     spot = lax.broadcasted_iota(i32, (width, LANES), 0)
-    held_iota = lax.broadcasted_iota(i32, (width, held), 1)
+    piece_held = held // FOLD
+    held_iota = lax.broadcasted_iota(i32, (width, piece_held), 1)
+
+    def side_by_side(table):
+        size = table.shape[0] // FOLD
+        return jnp.concatenate([table[f * size:(f + 1) * size] for f in range(FOLD)], axis=1)
+
+    def of_quarter(wide, which):
+        depth = wide.shape[1] // FOLD
+        value = wide[:, :depth]
+        for f in range(1, FOLD):
+            value = jnp.where(which == f, wide[:, f * depth:(f + 1) * depth], value)
+        return value
 
     def pick(q, _):
         slot_q = slots[pl.ds(pl.multiple_of(q * ROWS, ROWS), ROWS), :]
@@ -120,8 +134,9 @@
         for s in range(ROWS):
             total = total + jnp.where(slot_q[s:s + 1, :] == spot, id_q[s:s + 1, :], 0)
         chosen = jnp.sum(total.astype(f32), axis=1, keepdims=True).astype(i32)
-        hot = jnp.where(held_iota == chosen, 1.0, 0.0).astype(bf16)
-        picked = jnp.dot(hot, book[...], preferred_element_type=f32).astype(bf16)
+        hot = jnp.where(held_iota == chosen % piece_held, 1.0, 0.0).astype(bf16)
+        wide = jnp.dot(hot, side_by_side(book[...]), preferred_element_type=f32)
+        picked = of_quarter(wide, chosen // piece_held).astype(bf16)
         rows[q, pl.ds(pl.multiple_of(me * width, width), width), :] = picked
         for s in range(1, owners_x):
             x_copy(q, s).start()
@@ -135,13 +150,15 @@
     for load in loads[4:]:
         load.wait()
     levels = [bucket_ref[v] for v in range(bucket_ref.shape[0])]
-    place_iota = lax.broadcasted_iota(i32, (2 * ROWS, SUPER), 1)
+    piece_super = SUPER // FOLD
+    place_iota = lax.broadcasted_iota(i32, (2 * ROWS, piece_super), 1)
 
     def prepare(q, _):
         place_q = place[pl.ds(pl.multiple_of(q * ROWS, ROWS), ROWS), :]
         for l in range(0, LANES, 2):
             pair = jnp.concatenate([place_q[:, l:l + 1], place_q[:, l + 1:l + 2]], axis=0)
-            perm[q, l * ROWS:(l + 2) * ROWS, :] = jnp.where(place_iota == pair, 1.0, 0.0).astype(bf16)
+            perm[q, l * ROWS:(l + 2) * ROWS, :] = jnp.where(place_iota == pair % piece_super, 1.0, 0.0).astype(bf16)
+            quarter[q, l * ROWS:(l + 2) * ROWS, :] = jnp.broadcast_to(pair // piece_super, (2 * ROWS, LANES))
         for l in range(LANES):
             code = codes[pl.ds(q * SUPER + l, ROWS, stride=LANES), :]
             value = jnp.full(code.shape, levels[0], f32)
@@ -173,7 +190,7 @@
             top = None
             for p in range(0, BLOCK * ROWS, 128):
                 piece = dec[q, h * BLOCK * ROWS + p:h * BLOCK * ROWS + p + 128, :]
-                sim = lax.dot_general(piece, query, (((1,), (1,)), ((), ())), preferred_element_type=f32)
+                sim = jnp.dot(piece, query, preferred_element_type=f32)
                 sim = jnp.max(sim.reshape(-1, ROWS, sim.shape[1]), axis=0)
                 top = sim if top is None else jnp.maximum(top, sim)
             best[j, pl.ds(pl.multiple_of(q * 2 * ROWS + h * ROWS, ROWS), ROWS), :] = top
@@ -185,10 +202,11 @@
                     continue
                 source = lax.rem(x + s, owners_x) * cores + lax.rem(c + t, cores)
                 send(q, source, c_send.at[q, t], (y, z, x, c)).wait_recv()
-        vectors = jnp.dot(perm[q], rows[q], preferred_element_type=f32) + resid[q]
+        wide = jnp.dot(perm[q], side_by_side(rows[q]), preferred_element_type=f32)
+        vectors = of_quarter(wide, quarter[q]) + resid[q]
         squares = jnp.sum(vectors * vectors, axis=1, keepdims=True)
         dec[q] = (vectors * lax.rsqrt(squares + norm_eps)).astype(bf16)
-        score(z, q_ref[...], q)
+        score(z, panels[z], q)
         return 0
 
     lax.fori_loop(0, supers, decode, 0)
@@ -211,10 +229,12 @@
         lines = []
         for d in range(docs):
             lines.append(jnp.max(jnp.where(which == d, maxima, floor_value), axis=0, keepdims=True))
-        found = jnp.concatenate(lines, axis=0)
-        found = jnp.where(found > 0.5 * floor_value, found, 0.0)
+        tops = jnp.concatenate(lines, axis=0)
+        found[j] = jnp.where(tops > 0.5 * floor_value, tops, 0.0)
+
+    def total_up(j):
         total = lax.dot_general(
-            gather, found, (((1,), (1,)), ((), ())),
+            gather, found[j], (((1,), (1,)), ((), ())),
             preferred_element_type=f32, precision=lax.Precision.HIGHEST,
         )
         out_ref[j] = total * (1.0 / tokens)
@@ -224,7 +244,7 @@
     def panel(s, _):
         j = lax.rem(z + shards - s, shards)
         pltpu.make_async_remote_copy(
-            src_ref=q_ref, dst_ref=panels.at[j], send_sem=q_send.at[s], recv_sem=q_recv.at[j],
+            src_ref=panels.at[z], dst_ref=panels.at[j], send_sem=q_send.at[s], recv_sem=q_recv.at[j],
             device_id=(y, z, x, c), device_id_type=pl.DeviceIdType.MESH,
         ).wait_recv()
 
@@ -237,6 +257,9 @@
         return 0
 
     lax.fori_loop(1, shards, panel, 0)
+
+    for j in range(shards):
+        total_up(j)
 
     for s in range(1, shards):
         q_copy(s).wait_send()
@@ -282,11 +305,13 @@
             pltpu.VMEM((total // LANES, LANES), i32),
             pltpu.VMEM((total // LANES, LANES), i32),
             pltpu.VMEM((supers, SUPER, depth), bf16),
-            pltpu.VMEM((supers, SUPER, SUPER), bf16),
+            pltpu.VMEM((supers, SUPER, SUPER // FOLD), bf16),
+            pltpu.VMEM((supers, SUPER, depth), i32),
             pltpu.VMEM((supers, SUPER, depth), f32),
             pltpu.VMEM((supers, SUPER, depth), bf16),
-            pltpu.VMEM((shards, panel * tokens, depth), bf16),
+            pltpu.VMEM((shards, depth, panel * tokens), bf16),
             pltpu.VMEM((shards, total // BLOCK, panel * tokens), f32),
+            pltpu.VMEM((shards, docs, panel * tokens), f32),
             dma((8,)),
             dma((shards,)),
             dma((shards,)),

time: 29.7 us -> 26.1 us (0.88)
  Pallas kernels: 28.1 us -> 24.5 us
    pallas_call x1, Pallas kernels: 28.1 us -> 24.5 us  [local(): pl.pallas_call(functools.partial(kernel, shards, owners_x, cores), out_sh...]
where the time goes in v3:
time: 26.1 us; the launch traced here: 25.9 us
  Pallas kernels  24.5 us (94%)
  local copies, waits for them, and re-layouts  1.38 us (5%)
    pallas_call x1, Pallas kernels, local(): pl.pallas_call(functools.partial(kernel, shards, owners_x, cores), out_sh...  24.5 us
    unnamed x1, local copies, waits for them, and re-layouts  1.38 us

profile of v3, /device:TPU:0, one launch (start us, length us, event | category | flops | bytes accessed | tf_op | source)
XLA Modules:
  0.0 25.9 jit_solution(6012654538990984355)
XLA Ops:
  0.0 24.5 %rescore.1 = f32[4,16,16]{2,1,0:T(8,128)} custom-call(s32[32,128]{1,0:T(8,128)} %bitcast.4, s32[4,1,1,32]{3,2,1,0:T(1,128)} %cand_hbm.1, s32[4]{0:T(128)} %bitcast.5, s32[1,16]{1,0:T(1,128)} %docs_hbm.1, f32[4]{0:T(128)} %bucket_hbm.1, bf16[512,128]{1,0:T(8,128)(2,1)} %bitcast.3, bf16[4096,128]{1,0:T(8,128)(2,1)} %book_hbm.1, s32[4096,128]{1,0:T(8,128)} %codes_hbm.1), custom_call_target="tpu_custom_call" | custom-call | tf_op jit(solution)/shard_map/rescore/pallas_call | solution.py:290
  24.5 1.4 %copy.10 = f32[4,16,16]{2,1,0:T(8,128)} copy(f32[4,16,16]{2,1,0:T(8,128)} %rescore.1) | data formatting | bytes 8192

commit v4 on v3

--- a/solution.py
+++ b/solution.py
@@ -25,6 +25,7 @@
     ids_ref, cand_ref, counts_ref, docs_ref, bucket_ref, q_ref, book, codes, ranks, place, slots, rows, perm, quarter, resid, dec, panels, best, found,
     load_sem, q_send, q_recv, x_send, c_send, r_send, row_recv,
 ):
+    bits = [1 << n for n in range(shards.bit_length() - 1)]
     y, z = lax.axis_index("grp"), lax.axis_index("doc")
     x, c = lax.axis_index("qry"), lax.axis_index("dim")
     owners = owners_x * cores
@@ -59,11 +60,14 @@
     panels[z] = q_ref[...].T
     pl.semaphore_wait(barrier, len(peers))
 
+    def partner(s):
+        return sum(((z // bit + s // bit) % 2) * bit for bit in bits)
+
     def q_copy(s):
         return pltpu.make_async_remote_copy(
             src_ref=panels.at[z], dst_ref=panels.at[z],
             send_sem=q_send.at[s], recv_sem=q_recv.at[z],
-            device_id=(y, lax.rem(z + s, shards), x, c), device_id_type=pl.DeviceIdType.MESH,
+            device_id=(y, partner(s), x, c), device_id_type=pl.DeviceIdType.MESH,
         )
 
     for s in range(1, shards):
@@ -165,15 +169,23 @@
             for v in range(1, len(levels)):
                 value = jnp.where(code == v, levels[v], value)
             resid[q, l * ROWS:(l + 1) * ROWS, :] = value
+        return 0
+
+    def pass_on(q):
         for s in range(1, owners_x):
             source = lax.rem(x + s, owners_x) * cores + c
-            x_wait = send(q, source, x_send.at[q, s], (y, z, x, c))
-            x_wait.wait_recv()
+            send(q, source, x_send.at[q, s], (y, z, x, c)).wait_recv()
             for t in range(1, cores):
                 relay(q, s, t).start()
-        return 0
-
-    lax.fori_loop(0, supers, prepare, 0)
+
+    def prepare_and_pass(q, _):
+        prepare(q, 0)
+        pass_on(q - lead)
+        return 0
+
+    lead = min(2, supers)
+    lax.fori_loop(0, lead, prepare, 0)
+    lax.fori_loop(lead, supers, prepare_and_pass, 0)
 
     blocks = supers * 2 * ROWS
     line = lax.broadcasted_iota(i32, (blocks, 1), 0)
@@ -193,7 +205,14 @@
                 sim = jnp.dot(piece, query, preferred_element_type=f32)
                 sim = jnp.max(sim.reshape(-1, ROWS, sim.shape[1]), axis=0)
                 top = sim if top is None else jnp.maximum(top, sim)
-            best[j, pl.ds(pl.multiple_of(q * 2 * ROWS + h * ROWS, ROWS), ROWS), :] = top
+            at = q * 2 * ROWS + h * ROWS
+            best[j, pl.ds(at if isinstance(at, int) else pl.multiple_of(at, ROWS), ROWS), :] = top
+
+    def panel_arrival(j):
+        pltpu.make_async_remote_copy(
+            src_ref=panels.at[z], dst_ref=panels.at[j], send_sem=q_send.at[0], recv_sem=q_recv.at[j],
+            device_id=(y, z, x, c), device_id_type=pl.DeviceIdType.MESH,
+        ).wait_recv()
 
     def decode(q, _):
         for s in range(owners_x):
@@ -207,9 +226,18 @@
         squares = jnp.sum(vectors * vectors, axis=1, keepdims=True)
         dec[q] = (vectors * lax.rsqrt(squares + norm_eps)).astype(bf16)
         score(z, panels[z], q)
-        return 0
-
-    lax.fori_loop(0, supers, decode, 0)
+        score(near, panels[near], q)
+        return 0
+
+    def decode_and_pass(q, _):
+        decode(q, 0)
+        pass_on(q + supers - lead)
+        return 0
+
+    near = partner(1)
+    panel_arrival(near)
+    lax.fori_loop(0, lead, decode_and_pass, 0)
+    lax.fori_loop(lead, supers, decode, 0)
 
     panel_rows = q_ref.shape[0]
     queries = out_ref.shape[1]
@@ -242,21 +270,15 @@
     finish(z)
 
     def panel(s, _):
-        j = lax.rem(z + shards - s, shards)
-        pltpu.make_async_remote_copy(
-            src_ref=panels.at[z], dst_ref=panels.at[j], send_sem=q_send.at[s], recv_sem=q_recv.at[j],
-            device_id=(y, z, x, c), device_id_type=pl.DeviceIdType.MESH,
-        ).wait_recv()
-
-        def each(q, _):
+        j = partner(s)
+        panel_arrival(j)
+        for q in range(supers):
             score(j, panels[j], q)
-            return 0
-
-        lax.fori_loop(0, supers, each, 0)
-        finish(j)
-        return 0
-
-    lax.fori_loop(1, shards, panel, 0)
+        finish(partner(s - 1))
+        return 0
+
+    lax.fori_loop(2, shards, panel, 0)
+    finish(partner(shards - 1))
 
     for j in range(shards):
         total_up(j)

time: 26.1 us -> 22.8 us (0.87)
  Pallas kernels: 24.5 us -> 21.2 us
    pallas_call x1, Pallas kernels: 24.5 us -> 21.2 us  [local(): pl.pallas_call(functools.partial(kernel, shards, owners_x, cores), out_sh...]
where the time goes in v4:
time: 22.8 us; the launch traced here: 22.6 us
  Pallas kernels  21.2 us (93%)
  local copies, waits for them, and re-layouts  1.38 us (6%)
    pallas_call x1, Pallas kernels, local(): pl.pallas_call(functools.partial(kernel, shards, owners_x, cores), out_sh...  21.2 us
    unnamed x1, local copies, waits for them, and re-layouts  1.38 us

profile of v4, /device:TPU:0, one launch (start us, length us, event | category | flops | bytes accessed | tf_op | source)
XLA Modules:
  0.0 22.6 jit_solution(297209626222517033)
XLA Ops:
  0.0 21.2 %rescore.1 = f32[4,16,16]{2,1,0:T(8,128)} custom-call(s32[32,128]{1,0:T(8,128)} %bitcast.4, s32[4,1,1,32]{3,2,1,0:T(1,128)} %cand_hbm.1, s32[4]{0:T(128)} %bitcast.5, s32[1,16]{1,0:T(1,128)} %docs_hbm.1, f32[4]{0:T(128)} %bucket_hbm.1, bf16[512,128]{1,0:T(8,128)(2,1)} %bitcast.3, bf16[4096,128]{1,0:T(8,128)(2,1)} %book_hbm.1, s32[4096,128]{1,0:T(8,128)} %codes_hbm.1), custom_call_target="tpu_custom_call" | custom-call | tf_op jit(solution)/shard_map/rescore/pallas_call | solution.py:312
  21.2 1.4 %copy.10 = f32[4,16,16]{2,1,0:T(8,128)} copy(f32[4,16,16]{2,1,0:T(8,128)} %rescore.1) | data formatting | bytes 8192
